TPU v7x, 512 devices: a whole 4x4x16 slice. The times are simulated.
512 devices in a mesh: doc: 64 (over y, z), bin: 8 (over x, core).
Axes of the slice: x: 4, y: 4, z: 16, core: 2. Of those that a mesh axis runs over, the one named last changes fastest.
Arguments:
- profiles: float32 [8192, 8192], P('doc', 'bin'), may hold values from -6 to 6
- assign: int32 [8192], P('doc'), may hold values from 0 to 4095, as said below
Outputs:
- centroids: float32 [8, 512, 8192], P('bin', 'doc')
- scores: float32 [4096, 8192], P('bin', 'doc')
Inputs may be any that keep to these rules, and one draw needn't show every extreme that they name: `assign`: cluster k belongs to owner (k % 512) // 8. In each aligned block of 128 documents, at most 8 documents are assigned to the clusters of one owner, and some owner has exactly 8 of them.
All inputs are finite; a program needn't handle non-finite values.
Results may differ from a plain program's by a relative error of at most 0.0029.
Values may be sent and summed in bfloat16 or wider, within the bound.
A program may use at most 64 MiB of HBM per device.

v0:
```python
import jax
import jax.numpy as jnp
from jax import lax
from jax.sharding import PartitionSpec as P

K = 4096
norm_epsilon = 1e-06


def shards(profiles, assign):
    doc_devs = lax.axis_size("doc")
    bin_devs = lax.axis_size("bin")
    doc_count, slab_width = profiles.shape
    slice_width = K // bin_devs
    part_width = slice_width // doc_devs
    owned_count = part_width * bin_devs
    capacity = 4 * doc_count // doc_devs
    owner_rank = assign % slice_width // part_width
    local_index = assign // slice_width * part_width + assign % part_width
    owner_hits = (owner_rank[:, None] == jnp.arange(doc_devs, dtype=jnp.int32)[None, :]).astype(
        jnp.int32
    )
    slot_rank = jnp.sum(jnp.cumsum(owner_hits, axis=0) * owner_hits, axis=1) - 1
    slot_index = owner_rank * capacity + slot_rank
    send_rows = (
        jnp.zeros((doc_devs * capacity, slab_width), jnp.float32).at[slot_index].set(profiles)
    )
    send_ids = jnp.full((doc_devs * capacity,), -1, jnp.int32).at[slot_index].set(local_index)
    send_rows = send_rows.reshape(doc_devs, capacity, slab_width)
    send_ids = send_ids.reshape(doc_devs, capacity)
    got_rows, got_ids = (
        lax.all_to_all(send_rows, "doc", split_axis=0, concat_axis=0, tiled=True),
        lax.all_to_all(send_ids, "doc", split_axis=0, concat_axis=0, tiled=True),
    )
    member = (
        got_ids.reshape(-1)[None, :] == jnp.arange(owned_count, dtype=jnp.int32)[:, None]
    ).astype(jnp.float32)
    cluster_sums = jnp.dot(
        member,
        got_rows.reshape(-1, slab_width),
        precision=lax.Precision.HIGHEST,
        preferred_element_type=jnp.float32,
    )
    cluster_sums = cluster_sums.reshape(bin_devs, part_width, slab_width)
    partial_squares = jnp.sum(cluster_sums * cluster_sums, axis=2)
    total_squares = lax.psum(partial_squares, "bin")
    unit = cluster_sums * lax.rsqrt(total_squares + norm_epsilon)[:, :, None]
    centroids = lax.all_to_all(unit, "bin", split_axis=0, concat_axis=2, tiled=True)
    gathered = lax.all_gather(unit.astype(jnp.bfloat16), "doc", axis=1, tiled=True)
    panel_rows = gathered.reshape(-1, slab_width)
    doc_values = profiles.astype(jnp.bfloat16)
    scores = lax.psum_scatter(
        lax.dot_general(
            panel_rows, doc_values, (((1,), (1,)), ((), ())), preferred_element_type=jnp.float32
        ),
        "bin",
        scatter_dimension=0,
        tiled=True,
    )
    return (centroids, scores)


def solution(mesh):
    in_specs = (P("doc", "bin"), P("doc"))
    out_specs = (P("bin", "doc", None), P("bin", "doc"))
    return jax.shard_map(shards, mesh=mesh, in_specs=in_specs, out_specs=out_specs, check_vma=False)
```

profile of v0, /device:TPU:8, one launch (start us, length us, event | category | flops | bytes accessed | tf_op | source)
XLA Modules:
  0.0 360.2 jit_solution(9232095160435295296)
XLA Ops:
  7.2 0.7 fusion.12
  7.8 0.1 fusion.9
  7.9 0.2 reduce_window_sum.11
  8.1 0.2 select_reduce_fusion
  8.3 1.0 scatter_custom_fusion
  9.3 0.7 all_to_all.22
  10.0 18.7 %all-to-all-start = ((s32[64,1,8]{2,1,0:T(1,128)}), s32[64,1,8]{2,1,0:T(1,128)S(1)}, u32[]{:S(2)}, u32[]{:S(2)}) async-start(s32[64,1,8]{2,1,0:T(1,128)} %bitcast), calls=%async_computation | async-start | bytes 65536 | tf_op jit(solution)/shard_map/all_to_all | solution.py:33
  28.7 3.0 scatter_custom_fusion.1
  31.7 10.5 %all-to-all-done = s32[64,1,8]{2,1,0:T(1,128)S(1)} async-done(((s32[64,1,8]{2,1,0:T(1,128)}), s32[64,1,8]{2,1,0:T(1,128)S(1)}, u32[]{:S(2)}, u32[]{:S(2)}) %all-to-all-start) | async-done | bytes 2080 | tf_op jit(solution)/shard_map/all_to_all | solution.py:33
  42.2 5.6 %all-to-all-start.1 = ((f32[64,8,1024]{2,1,0:T(8,128)}), f32[64,8,1024]{2,1,0:T(8,128)S(1)}, u32[]{:S(2)}, u32[]{:S(2)}) async-start(f32[64,8,1024]{2,1,0:T(8,128)} %bitcast.1), calls=%async_computation.1 | async-start | bytes 4194304 | tf_op jit(solution)/shard_map/all_to_all | solution.py:32
  47.8 0.0 all-gather.2.cloned.1.call-start
  47.8 0.5 broadcast.71
  48.3 0.7 reduce.3
  49.1 0.1 eq.45
  49.2 95.7 %all-to-all-done.1 = f32[64,8,1024]{2,1,0:T(8,128)S(1)} async-done(((f32[64,8,1024]{2,1,0:T(8,128)}), f32[64,8,1024]{2,1,0:T(8,128)S(1)}, u32[]{:S(2)}, u32[]{:S(2)}) %all-to-all-start.1) | async-done | bytes 2097184 | tf_op jit(solution)/shard_map/all_to_all | solution.py:32
  144.9 1.0 multiply_reduce_fusion
  145.9 12.4 %psum.7 = f32[8,8]{1,0:T(8,128)S(1)} all-reduce(f32[8,8]{1,0:T(8,128)S(1)} %get-tuple-element.6), channel_id=1, replica_groups=mesh['doc'=64,'bin'=8] {'bin'}, use_global_device_ids=true, to_apply=%region_5.6 | all-reduce | flops 64 | bytes 512 | tf_op jit(solution)/shard_map/psum | solution.py:46
  158.3 0.8 fusion.13
  159.1 0.0 reduce-scatter.2.cloned.1.call-start
  159.2 149.0 %all-gather.2.cloned.1.call-done = bf16[8,512,1024]{2,1,0:T(8,128)(2,1)} async-done(((bf16[8,8,1024]{2,1,0:T(8,128)(2,1)}), bf16[8,512,1024]{2,1,0:T(8,128)(2,1)}) %all-gather.2.cloned.1.call-update) | async-done | bytes 8388624 | tf_op jit(solution)/shard_map/all_gather | solution.py:49
  308.1 7.1 %fusion.4 = f32[4096,128]{1,0:T(8,128)} fusion(bf16[4096,1024]{1,0:T(8,128)(2,1)} %bitcast.18, f32[128,1024]{1,0:T(8,128)S(1)} %copy-done), kind=kOutput, calls=%fused_computation.6 | convolution fusion | flops 1073872896 | bytes 11010048 | tf_op jit(solution)/shard_map/dot_general | solution.py:53
  315.3 11.6 %all_to_all.32 = f32[8,8,1024]{2,1,0:T(8,128)S(1)} all-to-all(f32[8,8,1024]{2,1,0:T(8,128)S(1)} %get-tuple-element.3), channel_id=1, replica_groups=mesh['doc'=64,'bin'=8] {'bin'}, dimensions={0} | all-to-all | bytes 524288 | tf_op jit(solution)/shard_map/all_to_all | solution.py:48
  326.9 25.8 %reduce-scatter.2.cloned.1.call-done = f32[512,128]{1,0:T(8,128)} async-done(((f32[4096,128]{1,0:T(8,128)}), f32[512,128]{1,0:T(8,128)}) %reduce-scatter.2.cloned.1.call-update) | async-done | bytes 262160 | tf_op jit(solution)/shard_map/reduce_scatter | solution.py:52
  352.7 0.7 copy.6
  (7 shorter events, 0.1 us)
Async XLA Ops:
  10.0 32.2 %all-to-all-start = ((s32[64,1,8]{2,1,0:T(1,128)}), s32[64,1,8]{2,1,0:T(1,128)S(1)}, u32[]{:S(2)}, u32[]{:S(2)}) async-start(s32[64,1,8]{2,1,0:T(1,128)} %bitcast), calls=%async_computation | async-start | bytes 65536 | tf_op jit(solution)/shard_map/all_to_all | solution.py:33
  42.2 102.7 %all-to-all-start.1 = ((f32[64,8,1024]{2,1,0:T(8,128)}), f32[64,8,1024]{2,1,0:T(8,128)S(1)}, u32[]{:S(2)}, u32[]{:S(2)}) async-start(f32[64,8,1024]{2,1,0:T(8,128)} %bitcast.1), calls=%async_computation.1 | async-start | bytes 4194304 | tf_op jit(solution)/shard_map/all_to_all | solution.py:32
  47.8 260.4 %copy-start = (f32[128,1024]{1,0:T(8,128)S(1)}, f32[128,1024]{1,0:T(8,128)}, u32[]{:S(2)}) copy-start(f32[128,1024]{1,0:T(8,128)} %param.2) | copy-start | bytes 1572868
  47.8 260.3 %all-gather.2.cloned.1.call-start = ((), (), s32[]{:S(2)}) async-start(), calls=%async_computation.4 | async-start | bytes 8519680 | tf_op jit(solution)/shard_map/all_gather | solution.py:49
  159.1 193.6 %reduce-scatter.2.cloned.1.call-start = ((), (), s32[]{:S(2)}) async-start(), calls=%async_computation.5 | async-start | bytes 2359296 | tf_op jit(solution)/shard_map/reduce_scatter | solution.py:52
Sparse Core Ops, SparseCore 0:
  159.2 148.8 all-gather.1
  315.4 37.2 reduce-scatter.1
where the time goes:
time: 361 us; the launch traced here: 360 us
  waiting for transfers between devices  281 us (78%)
  starting transfers between devices  24.4 us (7%)
  blocking collectives  24 us (7%)
  between operations  14.1 us (4%)
  matrix products  8.16 us (2%)
  local copies, waits for them, and re-layouts  5.95 us (2%)
    all_gather x1, waiting for transfers between devices, shards(): lax.all_gather(unit.astype(jnp.bfloat16), 'doc', axis=1, tiled=True)  149 us
    all_to_all x1, waiting for transfers between devices, shards(): lax.all_to_all(send_rows, 'doc', split_axis=0, concat_axis=0, tiled=True)  95.7 us
    reduce_scatter x1, waiting for transfers between devices, shards(): lax.psum_scatter(lax.dot_general(panel_rows, doc_values, (((1,), (1,)), (...  25.8 us
    all_to_all x1, starting transfers between devices, shards(): lax.all_to_all(send_ids, 'doc', split_axis=0, concat_axis=0, tiled=True)  18.7 us
    psum x1, blocking collectives, shards(): total_squares = lax.psum(partial_squares, 'bin')  12.4 us
    all_to_all x1, blocking collectives, shards(): lax.all_to_all(unit, 'bin', split_axis=0, concat_axis=2, tiled=True)  11.6 us
    all_to_all x1, waiting for transfers between devices, shards(): lax.all_to_all(send_ids, 'doc', split_axis=0, concat_axis=0, tiled=True)  10.5 us
  transfers between devices with their start and end apart: 4, of which 4 were waited for; matrix products, arithmetic and copies ran while one was open for 1% of the time, Pallas kernels for 0%

commit v1 on v0

--- a/solution.py
+++ b/solution.py
@@ -46,7 +46,10 @@
     total_squares = lax.psum(partial_squares, "bin")
     unit = cluster_sums * lax.rsqrt(total_squares + norm_epsilon)[:, :, None]
     centroids = lax.all_to_all(unit, "bin", split_axis=0, concat_axis=2, tiled=True)
-    gathered = lax.all_gather(unit.astype(jnp.bfloat16), "doc", axis=1, tiled=True)
+    gathered = jnp.concatenate(
+        lax.all_to_all(jnp.stack([unit.astype(jnp.bfloat16)] * lax.axis_size("doc")), "doc", 0, 0),
+        axis=1,
+    )
     panel_rows = gathered.reshape(-1, slab_width)
     doc_values = profiles.astype(jnp.bfloat16)
     scores = lax.psum_scatter(

time: 361 us -> 591 us (1.64)
  blocking collectives: 24 us -> 397 us
  waiting for transfers between devices: 281 us -> 130 us
  local copies, waits for them, and re-layouts: 5.95 us -> 15.1 us
    all_to_all x0 -> x1, blocking collectives: none -> 375 us  [shards(): lax.all_to_all(jnp.stack([unit.astype(jnp.bfloat16)] * lax.axis_size('doc...]
    all_gather x1 -> x0, waiting for transfers between devices: 149 us -> none  [shards(): lax.all_gather(unit.astype(jnp.bfloat16), 'doc', axis=1, tiled=True)]
    all_to_all x0 -> x1, local copies, waits for them, and re-layouts: none -> 8.06 us  [shards(): lax.all_to_all(jnp.stack([unit.astype(jnp.bfloat16)] * lax.axis_size('doc...]
  transfers between devices with their start and end apart: 4 -> 3, of which waited for: 4 -> 3; matrix products, arithmetic and copies ran while one was open for 1% -> 1% of each run, Pallas kernels for 0% -> 0%
where the time goes in v1:
time: 591 us
  blocking collectives  397 us (67%)
  waiting for transfers between devices  130 us (22%)
  starting transfers between devices  24.4 us (4%)
  local copies, waits for them, and re-layouts  15.1 us (3%)
  between operations  14.1 us (2%)
  matrix products  8.16 us (1%)
    all_to_all x1, blocking collectives, shards(): lax.all_to_all(jnp.stack([unit.astype(jnp.bfloat16)] * lax.axis_size('doc...  375 us
    all_to_all x1, waiting for transfers between devices, shards(): lax.all_to_all(send_rows, 'doc', split_axis=0, concat_axis=0, tiled=True)  95.7 us
    reduce_scatter x1, waiting for transfers between devices, shards(): lax.psum_scatter(lax.dot_general(panel_rows, doc_values, (((1,), (1,)), (...  23.8 us
    all_to_all x1, starting transfers between devices, shards(): lax.all_to_all(send_ids, 'doc', split_axis=0, concat_axis=0, tiled=True)  18.7 us
    psum x1, blocking collectives, shards(): total_squares = lax.psum(partial_squares, 'bin')  12.4 us
  transfers between devices with their start and end apart: 3, of which 3 were waited for; matrix products, arithmetic and copies ran while one was open for 1% of the time, Pallas kernels for 0%

profile of v1, /device:TPU:8, one launch (start us, length us, event | category | flops | bytes accessed | tf_op | source)
XLA Modules:
  0.0 591.0 jit_solution(4196521914417750470)
XLA Ops:
  7.2 0.7 fusion.12
  7.8 0.1 fusion.9
  7.9 0.2 reduce_window_sum.11
  8.1 0.2 select_reduce_fusion
  8.3 1.0 scatter_custom_fusion
  9.3 0.7 all_to_all.25
  10.0 18.7 %all-to-all-start = ((s32[64,1,8]{2,1,0:T(1,128)}), s32[64,1,8]{2,1,0:T(1,128)S(1)}, u32[]{:S(2)}, u32[]{:S(2)}) async-start(s32[64,1,8]{2,1,0:T(1,128)} %bitcast), calls=%async_computation | async-start | bytes 65536 | tf_op jit(solution)/shard_map/all_to_all | solution.py:33
  28.7 3.0 scatter_custom_fusion.1
  31.7 10.5 %all-to-all-done = s32[64,1,8]{2,1,0:T(1,128)S(1)} async-done(((s32[64,1,8]{2,1,0:T(1,128)}), s32[64,1,8]{2,1,0:T(1,128)S(1)}, u32[]{:S(2)}, u32[]{:S(2)}) %all-to-all-start) | async-done | bytes 2080 | tf_op jit(solution)/shard_map/all_to_all | solution.py:33
  42.2 5.6 all-to-all-start.1
  47.8 0.5 broadcast.73
  48.3 0.7 reduce.3
  49.1 0.1 eq.45
  49.1 95.7 %all-to-all-done.1 = f32[64,8,1024]{2,1,0:T(8,128)S(1)} async-done(((f32[64,8,1024]{2,1,0:T(8,128)}), f32[64,8,1024]{2,1,0:T(8,128)S(1)}, u32[]{:S(2)}, u32[]{:S(2)}) %all-to-all-start.1) | async-done | bytes 2097184 | tf_op jit(solution)/shard_map/all_to_all | solution.py:32
  144.9 1.0 multiply_reduce_fusion
  145.9 12.4 %psum.7 = f32[8,8]{1,0:T(8,128)S(1)} all-reduce(f32[8,8]{1,0:T(8,128)S(1)} %get-tuple-element.6), channel_id=1, replica_groups=mesh['doc'=64,'bin'=8] {'bin'}, use_global_device_ids=true, to_apply=%region_5.6 | all-reduce | flops 64 | bytes 512 | tf_op jit(solution)/shard_map/psum | solution.py:46
  158.3 0.1 fusion.13
  158.4 1.1 stack.2
  159.5 374.9 %all_to_all.37 = bf16[64,8,8,1024]{3,2,1,0:T(8,128)(2,1)} all-to-all(bf16[64,8,8,1024]{3,2,1,0:T(8,128)(2,1)S(1)} %stack.2), channel_id=1, replica_groups=mesh['doc'=64,'bin'=8] {'doc'}, dimensions={0} | all-to-all | bytes 16777216 | tf_op jit(solution)/shard_map/all_to_all | solution.py:50
  534.4 8.1 %copy.5 = bf16[64,8,8,1024]{3,2,0,1:T(8,128)(2,1)} copy(bf16[64,8,8,1024]{3,2,1,0:T(8,128)(2,1)} %all_to_all.37) | data formatting | bytes 16777216 | tf_op jit(solution)/shard_map/all_to_all | solution.py:50
  542.5 7.1 %fusion.4 = f32[4096,128]{1,0:T(8,128)} fusion(bf16[4096,1024]{1,0:T(8,128)(2,1)} %bitcast.20, f32[128,1024]{1,0:T(8,128)S(1)} %copy-done), kind=kOutput, calls=%fused_computation.6 | convolution fusion | flops 1073872896 | bytes 11010048 | tf_op jit(solution)/shard_map/dot_general | solution.py:56
  549.7 9.9 %all_to_all.38 = f32[8,8,1024]{2,1,0:T(8,128)S(1)} all-to-all(f32[8,8,1024]{2,1,0:T(8,128)S(1)} %get-tuple-element.3), channel_id=1, replica_groups=mesh['doc'=64,'bin'=8] {'bin'}, dimensions={0} | all-to-all | bytes 524288 | tf_op jit(solution)/shard_map/all_to_all | solution.py:48
  559.6 23.8 %reduce-scatter.2.cloned.1.call-done = f32[512,128]{1,0:T(8,128)} async-done(((f32[4096,128]{1,0:T(8,128)}), f32[512,128]{1,0:T(8,128)}) %reduce-scatter.2.cloned.1.call-update) | async-done | bytes 262160 | tf_op jit(solution)/shard_map/reduce_scatter | solution.py:55
  583.4 0.7 copy.7
  (7 shorter events, 0.1 us)
Async XLA Ops:
  10.0 32.2 %all-to-all-start = ((s32[64,1,8]{2,1,0:T(1,128)}), s32[64,1,8]{2,1,0:T(1,128)S(1)}, u32[]{:S(2)}, u32[]{:S(2)}) async-start(s32[64,1,8]{2,1,0:T(1,128)} %bitcast), calls=%async_computation | async-start | bytes 65536 | tf_op jit(solution)/shard_map/all_to_all | solution.py:33
  42.2 102.7 %all-to-all-start.1 = ((f32[64,8,1024]{2,1,0:T(8,128)}), f32[64,8,1024]{2,1,0:T(8,128)S(1)}, u32[]{:S(2)}, u32[]{:S(2)}) async-start(f32[64,8,1024]{2,1,0:T(8,128)} %bitcast.1), calls=%async_computation.1 | async-start | bytes 4194304 | tf_op jit(solution)/shard_map/all_to_all | solution.py:32
  47.8 535.7 %reduce-scatter.2.cloned.1.call-start = ((), (), s32[]{:S(2)}) async-start(), calls=%async_computation.5 | async-start | bytes 2359296 | tf_op jit(solution)/shard_map/reduce_scatter | solution.py:55
  534.4 8.1 %copy-start = (f32[128,1024]{1,0:T(8,128)S(1)}, f32[128,1024]{1,0:T(8,128)}, u32[]{:S(2)}) copy-start(f32[128,1024]{1,0:T(8,128)} %param.2) | copy-start | bytes 1572868
Sparse Core Ops, SparseCore 0:
  549.8 33.6 reduce-scatter.1
